TPU v7x, 256 devices: a whole 4x4x8 slice. The times are simulated.
256 devices in a mesh: lev: 8 (over z), wave: 32 (over x, y, core).
Axes of the slice: x: 4, y: 4, z: 8, core: 2. Of those that a mesh axis runs over, the one named last changes fastest.
Arguments:
- grid: bfloat16 [512, 512, 1024], P(None, 'wave', 'lev'), may hold values from -6 to 6
- legendre: bfloat16 [512, 512, 512], P('wave'), may hold values from -0.25 to 0.25
- lengths: int32 [512], replicated, may hold values from 256 to 1024, as said below
- lat_order: int32 [512], replicated, may hold values from 0 to 511, each once
- wave_order: int32 [512], replicated, may hold values from 0 to 511, each once
Outputs:
- spectral: bfloat16 [512, 512, 2, 512], P('lev', 'wave')
Inputs may be any that keep to these rules, and one draw needn't show every extreme that they name: `lengths`: at least 256, and 1024 on at least one latitude. `lat_order`: each latitude once. `wave_order`: each wavenumber once.
All inputs are finite; a program needn't handle non-finite values.
Results may differ from a plain program's by a relative error of at most 0.0058.
Values may be sent and summed in bfloat16 or wider, within the bound.
A program may use at most 128 MiB of HBM per device.

v0:
```python
import math

import jax
import jax.numpy as jnp
from jax import lax
from jax.sharding import PartitionSpec as P

NLAT = 512
NLON = 1024
TRUNC = 512


def trig_pair(phase, width):
    angle = 2.0 * math.pi * phase.astype(jnp.float32) / width
    return (jnp.cos(angle), jnp.sin(angle))


def row_table(length, wave_list, count):
    width = length.astype(jnp.float32)
    factor = 1.0 / jnp.sqrt(width)
    waves = wave_list[None, :]
    columns = jnp.arange(count, dtype=jnp.int32)
    highs = 32 * jnp.arange(count // 32, dtype=jnp.int32)
    lows = jnp.arange(32, dtype=jnp.int32)
    high_cos, high_sin = trig_pair(highs[:, None] * waves % length, width)
    low_cos, low_sin = trig_pair(lows[:, None] * waves % length, width)
    real = high_cos[:, None, :] * low_cos[None, :, :] - high_sin[:, None, :] * low_sin[None, :, :]
    imag = high_sin[:, None, :] * low_cos[None, :, :] + high_cos[:, None, :] * low_sin[None, :, :]
    real = real.reshape(count, wave_list.shape[0])
    imag = imag.reshape(count, wave_list.shape[0])
    inside = columns[:, None] < length
    cosines = jnp.where(inside, real * factor, 0.0)
    sines = jnp.where(inside, -imag * factor, 0.0)
    return jnp.concatenate([cosines, sines], axis=1).astype(jnp.bfloat16)


def on_device(grid, legendre, lengths, lat_order, wave_order):
    lat_count = grid.shape[1]
    field_count = grid.shape[0] // lax.axis_size("lev")
    slot_count = legendre.shape[0]
    row_lengths = lengths[lat_order]
    own_lengths = lax.dynamic_slice_in_dim(
        row_lengths, lax.axis_index("wave") * lat_count, lat_count
    )
    latitudes = jnp.arange(lat_count, dtype=jnp.int32)
    full_rows = lax.all_to_all(grid, "lev", split_axis=0, concat_axis=2, tiled=True)

    def one_latitude(position):
        block = lax.dynamic_index_in_dim(full_rows, position, 1, keepdims=False)
        length = lax.dynamic_index_in_dim(own_lengths, position, 0, keepdims=False)
        table = row_table(length, wave_order, NLON)
        return jnp.dot(block, table, preferred_element_type=jnp.float32)

    fourier = lax.map(one_latitude, latitudes).astype(jnp.bfloat16)
    fourier = fourier.reshape(lat_count, field_count, 2, TRUNC)
    inverse = jnp.zeros((NLAT,), jnp.int32).at[lat_order].set(jnp.arange(NLAT, dtype=jnp.int32))
    own_waves = lax.dynamic_slice_in_dim(
        wave_order, lax.axis_index("wave") * slot_count, slot_count
    )
    upper_part = jnp.arange(TRUNC, dtype=jnp.int32)[None, :] >= own_waves[:, None]
    arrived = lax.all_to_all(fourier, "wave", split_axis=3, concat_axis=0, tiled=True)
    ordered = jnp.take(arrived, inverse, axis=0)
    total = jnp.einsum("lkcs,sln->kscn", ordered, legendre, preferred_element_type=jnp.float32)
    return jnp.where(upper_part[None, :, None, :], total, 0.0).astype(jnp.bfloat16)


def solution(mesh):
    return jax.shard_map(
        on_device,
        mesh=mesh,
        in_specs=(P(None, "wave", "lev"), P("wave", None, None), P(), P(), P()),
        out_specs=P("lev", "wave", None, None),
        check_vma=False,
    )
```

profile of v0, /device:TPU:1, one launch (start us, length us, event | category | flops | bytes accessed | tf_op | source)
XLA Modules:
  0.0 312.8 jit_solution(11385610202020372256)
XLA Ops:
  0.0 9.1 %all-to-all-start = ((bf16[512,16,128]{2,1,0:T(8,128)(2,1)}), bf16[512,16,128]{2,1,0:T(8,128)(2,1)S(1)}, u32[]{:S(2)}, u32[]{:S(2)}) async-start(bf16[512,16,128]{2,1,0:T(8,128)(2,1)} %param.7), calls=%async_computation | async-start | bytes 4194304 | tf_op jit(solution)/shard_map/all_to_all | solution.py:46
  9.2 3.5 %gather_fusion = s32[512]{0:T(512)S(1)} fusion(s32[512]{0:T(512)S(1)} %copy-done, s32[1024]{0:T(1024)S(1)} %pad_clamp_fusion.1), kind=kCustom, calls=%fused_computation | custom fusion | bytes 6144 | tf_op jit(solution)/shard_map/gather | solution.py:41
  12.8 44.8 %all-to-all-done = bf16[512,16,128]{2,1,0:T(8,128)(2,1)S(1)} async-done(((bf16[512,16,128]{2,1,0:T(8,128)(2,1)}), bf16[512,16,128]{2,1,0:T(8,128)(2,1)S(1)}, u32[]{:S(2)}, u32[]{:S(2)}) %all-to-all-start) | async-done | bytes 2097184 | tf_op jit(solution)/shard_map/all_to_all | solution.py:46
  57.6 2.7 copy.30
  60.3 2.8 all_to_all.29
  63.1 159.0 %while.10 = (s32[]{:T(128)}, bf16[16,64,1024]{2,1,0:T(8,128)(2,1)}, s32[16]{0:T(128)S(1)}, bf16[64,16,1024]{2,0,1:T(8,128)(2,1)S(1)}, s32[16]{0:T(128)S(1)}, /*i...) while((s32[]{:T(128)}, bf16[16,64,1024]{2,1,0:T(8,128)(2,1)}, s32[16]{0:T(128)S(1)}, ...), condition=%wide.region_2.3_spmd, body=%wide.region_1.2_spmd.sunk | while | flops 145589280 | bytes 9311195 | solution.py:54
  68.2 1.8 fusion.51
  78.1 1.8 fusion.51
  88.1 1.8 fusion.51
  98.0 1.8 fusion.51
  107.9 1.8 fusion.51
  117.9 1.8 fusion.51
  127.8 1.8 fusion.51
  137.7 1.8 fusion.51
  147.7 1.8 fusion.51
  177.5 1.8 fusion.51
  187.4 1.8 fusion.51
  197.3 1.8 fusion.51
  207.3 1.8 fusion.51
  222.1 3.3 %reshape.159 = bf16[16,64,2,512]{3,2,1,0:T(2,128)(2,1)S(1)} reshape(bf16[16,64,1024]{2,1,0:T(8,128)(2,1)} %get-tuple-element.37) | data formatting | bytes 4194304 | tf_op jit(solution)/shard_map/reshape | solution.py:55
  225.4 8.3 %copy.19 = bf16[16,64,2,512]{1,2,0,3:T(2,128)(2,1)} copy(bf16[16,64,2,512]{3,2,1,0:T(2,128)(2,1)S(1)} %reshape.159) | data formatting | bytes 4194304 | tf_op jit(solution)/shard_map/reshape | solution.py:55
  233.8 9.8 %reshape.190 = bf16[32,2,16384]{2,1,0:T(2,128)(2,1)} reshape(bf16[512,16,2,64]{3,2,1,0:T(2,128)(2,1)} %bitcast.51) | data formatting | bytes 4194304
  243.6 10.8 %all-to-all-start.1 = ((bf16[32,2,16384]{2,1,0:T(2,128)(2,1)}), bf16[32,2,16384]{2,1,0:T(2,128)(2,1)S(1)}, u32[]{:S(2)}, u32[]{:S(2)}) async-start(bf16[32,2,16384]{2,1,0:T(2,128)(2,1)} %reshape.190), calls=%async_computation.1 | async-start | bytes 4194304 | tf_op jit(solution)/shard_map/all_to_all | solution.py:61
  254.5 2.6 scatter_custom_fusion
  257.2 25.5 %all-to-all-done.1 = bf16[32,2,16384]{2,1,0:T(2,128)(2,1)S(1)} async-done(((bf16[32,2,16384]{2,1,0:T(2,128)(2,1)}), bf16[32,2,16384]{2,1,0:T(2,128)(2,1)S(1)}, u32[]{:S(2)}, u32[]{:S(2)}) %all-to-all-start.1) | async-done | bytes 2097184 | tf_op jit(solution)/shard_map/all_to_all | solution.py:61
  282.7 4.0 %reshape.191 = bf16[512,16,2,64]{3,2,1,0:T(2,128)(2,1)} reshape(bf16[32,2,16384]{2,1,0:T(2,128)(2,1)S(1)} %all-to-all-done.1) | data formatting | bytes 4194304
  286.7 3.8 %copy.20 = bf16[16,64,2,512]{1,3,2,0:T(8,128)(2,1)S(1)} copy(bf16[16,64,2,512]{1,2,0,3:T(2,128)(2,1)} %bitcast.52) | data formatting | bytes 4194304 | tf_op jit(solution)/shard_map/all_to_all | solution.py:61
  290.5 3.1 %copy.21 = bf16[32,16,64,2,16]{2,4,3,1,0:T(8,128)(2,1)} copy(bf16[32,16,64,2,16]{2,4,0,3,1:T(8,128)(2,1)S(1)} %bitcast.53) | data formatting | bytes 4194304 | tf_op jit(solution)/shard_map/all_to_all | solution.py:61
  293.6 5.4 %gather_fusion.1 = bf16[512,64,2,16]{1,3,2,0:T(8,128)(2,1)} fusion(bf16[512,64,2,16]{1,3,2,0:T(8,128)(2,1)} %bitcast.50, s32[1024]{0:T(1024)S(1)} %pad_clamp_fusion), kind=kCustom, calls=%fused_computation.1 | custom fusion | bytes 4196352 | tf_op jit(solution)/shard_map/jit(_take)/gather | solution.py:62
  299.0 3.2 %broadcast_select_fusion = bf16[512,64,2,16]{1,3,2,0:T(8,128)(2,1)S(1)} fusion(bf16[512,64,2,16]{1,3,2,0:T(8,128)(2,1)} %gather_fusion.1, pred[512]{0:T(512)(128)(4,1)S(1)} %compare_and_fusion), kind=kLoop, calls=%fused_computation.47 | loop fusion | flops 1048576 | bytes 4194816 | tf_op jit(solution)/shard_map/jit(_take)/select_n | solution.py:62
  302.3 7.0 %fusion.37 = bf16[64,16,2,512]{3,0,2,1:T(8,128)(2,1)S(1)} fusion(pred[16,512]{1,0:T(8,128)(4,1)S(1)} %iota_compare_fusion.1, bf16[16,512,512]{2,1,0:T(8,128)(2,1)} %param.8, bf16[512,64,2,16]{1,3,2,0:T(8,128)(2,1)S(1)} %broadcast_select_fusion), kind=kOutput, calls=%fused_computation.48 | convolution fusion | flops 1075838976 | bytes 12591104 | tf_op jit(solution)/shard_map/lkcs,sln->kscn/dot_general | solution.py:63
  309.3 3.5 %copy.23 = bf16[64,16,2,512]{3,2,1,0:T(2,128)(2,1)} copy(bf16[64,16,2,512]{3,0,2,1:T(8,128)(2,1)S(1)} %fusion.37) | data formatting | bytes 4194304 | tf_op jit(solution)/shard_map/convert_element_type | solution.py:64
  (132 shorter events, 74.2 us)
Async XLA Ops:
  0.0 9.2 %copy-start = (s32[512]{0:T(512)S(1)}, s32[512]{0:T(512)}, u32[]{:S(2)}) copy-start(s32[512]{0:T(512)} %param.9) | copy-start | bytes 6148
  0.0 9.2 %copy-start.2 = (s32[512]{0:T(512)S(1)}, s32[512]{0:T(512)}, u32[]{:S(2)}) copy-start(s32[512]{0:T(512)} %param.10) | copy-start | bytes 6148
  0.0 57.6 %all-to-all-start = ((bf16[512,16,128]{2,1,0:T(8,128)(2,1)}), bf16[512,16,128]{2,1,0:T(8,128)(2,1)S(1)}, u32[]{:S(2)}, u32[]{:S(2)}) async-start(bf16[512,16,128]{2,1,0:T(8,128)(2,1)} %param.7), calls=%async_computation | async-start | bytes 4194304 | tf_op jit(solution)/shard_map/all_to_all | solution.py:46
  60.3 2.9 copy-start.1
  243.6 39.1 %all-to-all-start.1 = ((bf16[32,2,16384]{2,1,0:T(2,128)(2,1)}), bf16[32,2,16384]{2,1,0:T(2,128)(2,1)S(1)}, u32[]{:S(2)}, u32[]{:S(2)}) async-start(bf16[32,2,16384]{2,1,0:T(2,128)(2,1)} %reshape.190), calls=%async_computation.1 | async-start | bytes 4194304 | tf_op jit(solution)/shard_map/all_to_all | solution.py:61
where the time goes:
time: 314 us; the launch traced here: 313 us
  local copies, waits for them, and re-layouts  73.4 us (23%)
  waiting for transfers between devices  70.3 us (22%)
  other arithmetic  62.3 us (20%)
  loops' own time  61.5 us (20%)
  matrix products  25.2 us (8%)
  starting transfers between devices  20 us (6%)
    another operation x1, loops' own time, on_device(): fourier = lax.map(one_latitude, latitudes).astype(jnp.bfloat16)  61.5 us
    all_to_all x1, waiting for transfers between devices, on_device(): lax.all_to_all(grid, 'lev', split_axis=0, concat_axis=2, tiled=True)  44.8 us
    cos x16, other arithmetic, trig_pair(): return (jnp.cos(angle), jnp.sin(angle))  29.1 us
    all_to_all x1, waiting for transfers between devices, on_device(): lax.all_to_all(fourier, 'wave', split_axis=3, concat_axis=0, tiled=True)  25.5 us
    dot_general x16, matrix products, one_latitude(): return jnp.dot(block, table, preferred_element_type=jnp.float32)  18.2 us
    unnamed x8, local copies, waits for them, and re-layouts  13.9 us
    mul x16, other arithmetic, row_table(): cosines = jnp.where(inside, real * factor, 0.0)  12.5 us
    reshape x2, local copies, waits for them, and re-layouts, on_device(): fourier = fourier.reshape(lat_count, field_count, 2, TRUNC)  11.6 us
  transfers between devices with their start and end apart: 2, of which 2 were waited for; matrix products, arithmetic and copies ran while one was open for 2% of the time, Pallas kernels for 0%

commit v1 on v0

v1 whole, which is shorter than its diff:
```python
import functools
import math

import jax
import jax.numpy as jnp
from jax import lax
from jax.experimental import pallas as pl
from jax.experimental.pallas import tpu as pltpu
from jax.sharding import PartitionSpec as P

MESH = pl.DeviceIdType.MESH
BF16 = jnp.bfloat16
F32 = jnp.float32

LEVS = 8
WAVES = 32
ROWS = 16
SLOTS = 16
KEEP = 64
NLAT = 512
DEG = 512
NWAVE = 512
LANES = 128

CHUNKS = (4, 4, 4, 2, 2)
STARTS = tuple(sum(CHUNKS[:i]) for i in range(len(CHUNKS)))
LAST = len(CHUNKS) - 1
ZORDER = (4, 3, 5, 2, 6, 1, 7)

SIN_C = tuple((-1) ** i * math.pi ** (2 * i + 1) / math.factorial(2 * i + 1) for i in range(7))
COS_C = tuple((-1) ** i * math.pi ** (2 * i) / math.factorial(2 * i) for i in range(8))


def iota(shape, dim):
    return lax.broadcasted_iota(jnp.int32, shape, dim)


def horner(coefs, u):
    acc = jnp.full_like(u, coefs[-1])
    for c in coefs[-2::-1]:
        acc = acc * u + c
    return acc


def turn(count, width, inverse):
    whole = jnp.floor(count * inverse + 0.5)
    t = (count - whole * width) * inverse
    u = t * t
    s = t * horner(SIN_C, u)
    c = horner(COS_C, u)
    return 1.0 - 2.0 * s * s, 2.0 * s * c


def nt_dot(a, b):
    return lax.dot_general(a, b, (((1,), (1,)), ((), ())), preferred_element_type=F32)


def dot(a, b):
    return jnp.dot(a, b, preferred_element_type=F32)


def kernel(grid_hbm, leg_hbm, len_s, lat_s, wave_s, lat_v, wave_v, out_ref,
           gin, g, x, table, fs, fr, a, lraw, lp, acc, onehot, swap, mcol,
           gin_sem, leg_sem, zs, zr, ws, wr):
    z = lax.axis_index("lev")
    w = lax.axis_index("wave")
    bar = pltpu.get_barrier_semaphore()

    def signal_z(i, carry):
        pl.semaphore_signal(bar, inc=1, device_id=(lax.rem(z + i, LEVS), w), device_id_type=MESH)
        return carry

    def signal_w(i, carry):
        pl.semaphore_signal(bar, inc=1, device_id=(z, lax.rem(w + i, WAVES)), device_id_type=MESH)
        return carry

    lax.fori_loop(1, LEVS, signal_z, 0)
    lax.fori_loop(1, WAVES, signal_w, 0)
    grid_copy = pltpu.make_async_copy(grid_hbm, gin, gin_sem)
    grid_copy.start()
    leg_copy = pltpu.make_async_copy(leg_hbm, lraw, leg_sem)
    leg_copy.start()

    i = iota((256, 256), 0)
    j = iota((256, 256), 1)
    swap[...] = jnp.where(j == (i % 16) * 16 + i // 16, 1.0, 0.0).astype(BF16)

    grid_copy.wait()

    def to_rows(blk, carry):
        k0 = pl.multiple_of(blk * 16, 16)
        v = gin[pl.ds(k0, 16)].reshape(256, LANES)
        v = dot(swap[...], v).astype(BF16).reshape(16, 16, LANES)
        d = blk // 4
        kk = pl.multiple_of(lax.rem(blk, 4) * 16, 16)
        for c, rows in enumerate(CHUNKS):
            r0 = STARTS[c]
            g[pl.ds(LEVS * r0 + d * rows, rows), pl.ds(kk, 16), :] = v[r0 : r0 + rows]
        return carry

    lax.fori_loop(0, 32, to_rows, 0)
    pl.semaphore_wait(bar, LEVS - 1 + WAVES - 1)

    for c, rows in enumerate(CHUNKS):
        base = LEVS * STARTS[c]
        for o in ZORDER:
            p = lax.rem(z + o, LEVS)
            pltpu.make_async_remote_copy(
                src_ref=g.at[pl.ds(base + p * rows, rows)],
                dst_ref=x.at[pl.ds(base + z * rows, rows)],
                send_sem=zs.at[c], recv_sem=zr.at[c],
                device_id=(p, w), device_id_type=MESH,
            ).start()
    for c, rows in enumerate(CHUNKS):
        own = pl.ds(LEVS * STARTS[c] + z * rows, rows)
        x[own] = g[own]

    col = jnp.zeros((NWAVE, LANES), F32)
    for t in range(4):
        hit = iota((NWAVE, LANES), 1) + LANES * t == iota((NWAVE, LANES), 0)
        col = col + jnp.where(hit, wave_v[t : t + 1, :].astype(F32), 0.0)
    mcol[...] = jnp.broadcast_to(jnp.sum(col, axis=1, keepdims=True), (NWAVE, LANES))
    for c, rows in enumerate(CHUNKS):
        n = WAVES * rows
        q = iota((n, LANES), 0)
        row = (q // rows) * ROWS + STARTS[c] + q % rows
        col = jnp.zeros((n, LANES), F32)
        for t in range(4):
            hit = iota((n, LANES), 1) + LANES * t == row
            col = col + jnp.where(hit, lat_v[t : t + 1, :].astype(F32), 0.0)
        lat = jnp.sum(col, axis=1, keepdims=True)
        onehot[WAVES * STARTS[c] : WAVES * STARTS[c] + n, :] = jnp.where(
            iota((n, NLAT), 1).astype(F32) == lat, 1.0, 0.0
        ).astype(BF16)

    def make_table(r0, rows):
        def one(rr, carry):
            length = len_s[lat_s[w * ROWS + r0 + rr]]
            width = jnp.full((1, LANES), length, jnp.int32).astype(F32)
            inverse = 1.0 / width
            factor = 1.0 / jnp.sqrt(width)

            def block(b, carry2):
                s0 = pl.multiple_of(b * 64, 64)
                m = mcol[pl.ds(s0, 64), :]
                low = iota((64, LANES), 1).astype(F32)
                c0, s0_ = turn(m * low, width, inverse)
                dc, ds = turn(m * float(LANES), width, inverse)
                c0 = c0 * factor
                s0_ = s0_ * (-factor)
                c1 = c0 * dc + s0_ * ds
                s1 = s0_ * dc - c0 * ds
                two = 2.0 * dc
                for d in range(LEVS):
                    table[rr, pl.ds(s0, 64), d * LANES : (d + 1) * LANES] = c0.astype(BF16)
                    table[rr, pl.ds(s0, 64), (LEVS + d) * LANES : (LEVS + d + 1) * LANES] = s0_.astype(BF16)
                    if d < LEVS - 1:
                        c0, c1 = c1, two * c1 - c0
                        s0_, s1 = s1, two * s1 - s0_
                return carry2

            lax.fori_loop(0, NWAVE // 64, block, 0)
            return carry

        lax.fori_loop(0, rows, one, 0)

    def transform(r0, rows):
        def one(rr, carry):
            length = len_s[lat_s[w * ROWS + r0 + rr]]
            parts = []
            for d in range(LEVS):
                inside = iota((KEEP, LANES), 1) + d * LANES < length
                keep = jnp.where(inside, 1.0, 0.0).astype(BF16)
                parts.append(x[LEVS * r0 + d * rows + rr] * keep)
            line = jnp.concatenate(parts, axis=1)
            zero = jnp.zeros_like(line)
            real = jnp.concatenate([line, zero], axis=0)
            imag = jnp.concatenate([zero, line], axis=0)
            f = nt_dot(table[rr, :, : LEVS * LANES], real)
            f = f + nt_dot(table[rr, :, LEVS * LANES :], imag)
            f = f.astype(BF16)
            for p in range(WAVES):
                fs[WAVES * r0 + p * rows + rr] = f[SLOTS * p : SLOTS * (p + 1)]
            return carry

        lax.fori_loop(0, rows, one, 0)

    def send_wave(c):
        rows = CHUNKS[c]
        base = WAVES * STARTS[c]

        def one(o, carry):
            px = lax.rem(w // 8 + o // 8, 4)
            py = lax.rem(lax.rem(w // 2, 4) + lax.rem(o // 2, 4), 4)
            pc = lax.rem(lax.rem(w, 2) + lax.rem(o, 2), 2)
            p = px * 8 + py * 2 + pc
            pltpu.make_async_remote_copy(
                src_ref=fs.at[pl.ds(base + p * rows, rows)],
                dst_ref=fr.at[pl.ds(base + w * rows, rows)],
                send_sem=ws.at[c], recv_sem=wr.at[c],
                device_id=(z, p), device_id_type=MESH,
            ).start()
            return carry

        lax.fori_loop(1, WAVES, one, 0)
        own = pl.ds(base + w * rows, rows)
        fr[own] = fs[own]

    def z_all(c):
        region = pl.ds(LEVS * STARTS[c], (LEVS - 1) * CHUNKS[c])
        return pltpu.make_async_remote_copy(
            src_ref=g.at[region], dst_ref=x.at[region], send_sem=zs.at[c], recv_sem=zr.at[c],
            device_id=(lax.rem(z + 1, LEVS), w), device_id_type=MESH)

    def wave_all(c):
        region = pl.ds(WAVES * STARTS[c], (WAVES - 1) * CHUNKS[c])
        return pltpu.make_async_remote_copy(
            src_ref=fs.at[region], dst_ref=fr.at[region], send_sem=ws.at[c], recv_sem=wr.at[c],
            device_id=(z, lax.rem(w + 1, WAVES)), device_id_type=MESH)

    def to_slots(c):
        first = WAVES * STARTS[c] // 16

        def one(b, carry):
            q = pl.multiple_of(b * 16, 16)
            v = fr[pl.ds(q, 16)].reshape(256, LANES)
            a[:, pl.ds(q, 16), :] = dot(swap[...], v).astype(BF16).reshape(16, 16, LANES)
            return carry

        lax.fori_loop(first, first + 2 * CHUNKS[c], one, 0)

    make_table(0, CHUNKS[0])

    leg_copy.wait()

    def order_legendre(s, carry):
        m = wave_s[w * SLOTS + s]
        for h in range(2):
            cols = slice(256 * h, 256 * (h + 1))
            keep = iota((256, 256), 1) + 256 * h >= m
            for q in range(2):
                rows = slice(256 * q, 256 * (q + 1))
                v = dot(onehot[rows, :], lraw[s, :, cols])
                lp[s, rows, cols] = jnp.where(keep, v, 0.0).astype(BF16)
        return carry

    lax.fori_loop(0, SLOTS, order_legendre, 0)

    for c in range(len(CHUNKS)):
        z_all(c).wait_recv()
        transform(STARTS[c], CHUNKS[c])
        send_wave(c)
        if c < LAST:
            make_table(STARTS[c + 1], CHUNKS[c + 1])
        if c > 0:
            wave_all(c - 1).wait_recv()
            to_slots(c - 1)

    i = iota((LANES, LANES), 0)
    j = iota((LANES, LANES), 1)
    order = jnp.where(j == (i % 2) * KEEP + i // 2, 1.0, 0.0).astype(BF16)
    cut = WAVES * STARTS[LAST]

    def sum_first(s, carry):
        at = nt_dot(order, a[s, :cut, :]).astype(BF16)
        acc[s] = dot(at, lp[s, :cut, :])
        return carry

    lax.fori_loop(0, SLOTS, sum_first, 0)

    wave_all(LAST).wait_recv()
    to_slots(LAST)

    def sum_last(s, carry):
        at = nt_dot(order, a[s, cut:, :]).astype(BF16)
        total = acc[s] + dot(at, lp[s, cut:, :])
        out_ref[:, s] = total.astype(BF16).reshape(KEEP, 2, DEG)
        return carry

    lax.fori_loop(0, SLOTS, sum_last, 0)

    for c in range(len(CHUNKS)):
        z_all(c).wait_send()
        wave_all(c).wait_send()


def on_device(grid, legendre, lengths, lat_order, wave_order):
    any_spec = pl.BlockSpec(memory_space=pl.ANY)
    smem = pl.BlockSpec(memory_space=pltpu.SMEM)
    vmem = pl.BlockSpec(memory_space=pltpu.VMEM)
    n = len(CHUNKS)
    dma = pltpu.SemaphoreType.DMA
    return pl.pallas_call(
        kernel,
        out_shape=jax.ShapeDtypeStruct((KEEP, SLOTS, 2, DEG), BF16),
        in_specs=[any_spec, any_spec, smem, smem, smem, vmem, vmem],
        out_specs=vmem,
        scratch_shapes=[
            pltpu.VMEM((512, ROWS, LANES), BF16),
            pltpu.VMEM((LEVS * ROWS, KEEP, LANES), BF16),
            pltpu.VMEM((LEVS * ROWS, KEEP, LANES), BF16),
            pltpu.VMEM((max(CHUNKS), NWAVE, 2 * LEVS * LANES), BF16),
            pltpu.VMEM((WAVES * ROWS, SLOTS, LANES), BF16),
            pltpu.VMEM((WAVES * ROWS, SLOTS, LANES), BF16),
            pltpu.VMEM((SLOTS, NLAT, LANES), BF16),
            pltpu.VMEM((SLOTS, NLAT, DEG), BF16),
            pltpu.VMEM((SLOTS, NLAT, DEG), BF16),
            pltpu.VMEM((SLOTS, LANES, DEG), F32),
            pltpu.VMEM((NLAT, NLAT), BF16),
            pltpu.VMEM((256, 256), BF16),
            pltpu.VMEM((NWAVE, LANES), F32),
            dma, dma, dma((n,)), dma((n,)), dma((n,)), dma((n,)),
        ],
        compiler_params=pltpu.CompilerParams(
            collective_id=0, has_side_effects=True, vmem_limit_bytes=58 << 20
        ),
        cost_estimate=pl.CostEstimate(flops=14 * 10**9, bytes_accessed=14 << 20, transcendentals=0),
    )(grid, legendre, lengths, lat_order, wave_order, lat_order.reshape(4, 128), wave_order.reshape(4, 128))


def solution(mesh):
    return jax.shard_map(
        on_device,
        mesh=mesh,
        in_specs=(P(None, "wave", "lev"), P("wave", None, None), P(), P(), P()),
        out_specs=P("lev", "wave", None, None),
        check_vma=False,
    )
```

time: 314 us -> 91.9 us (0.29)
  Pallas kernels: 0 us -> 85.7 us
  waiting for transfers between devices: 70.3 us -> 0 us
  local copies, waits for them, and re-layouts: 73.4 us -> 6.02 us
  other arithmetic: 62.3 us -> 0 us
  loops' own time: 61.5 us -> 0 us
  matrix products: 25.2 us -> 0 us
  starting transfers between devices: 20 us -> 0 us
    pallas_call x0 -> x1, Pallas kernels: none -> 85.7 us  [on_device(): pl.pallas_call(kernel, out_shape=jax.ShapeDtypeStruct((KEEP, SLOTS, 2, DE...]
    all_to_all x2 -> x0, waiting for transfers between devices: 70.3 us -> none  [the longest x1 44.8 us: on_device(): lax.all_to_all(grid, 'lev', split_axis=0, concat_axis=2, tiled=True)]
    another operation x1 -> x0, loops' own time: 61.5 us -> none  [on_device(): fourier = lax.map(one_latitude, latitudes).astype(jnp.bfloat16)]
    cos x16 -> x0, other arithmetic: 29.1 us -> none  [trig_pair(): return (jnp.cos(angle), jnp.sin(angle))]
    dot_general x17 -> x0, matrix products: 25.2 us -> none  [the longest x16 18.2 us: one_latitude(): return jnp.dot(block, table, preferred_element_type=jnp.float32)]
    dynamic_slice x34 -> x0, local copies, waits for them, and re-layouts: 20.5 us -> none  [the longest x16 10.2 us: one_latitude(): length = lax.dynamic_index_in_dim(own_lengths, position, 0, keepdims=False)]
    all_to_all x2 -> x0, starting transfers between devices: 20 us -> none  [the longest x1 10.8 us: on_device(): lax.all_to_all(fourier, 'wave', split_axis=3, concat_axis=0, tiled=True)]
    mul x32 -> x0, other arithmetic: 12.5 us -> none  [the longest x16 12.5 us: row_table(): cosines = jnp.where(inside, real * factor, 0.0)]
  transfers between devices with their start and end apart: 2 -> 0, of which waited for: 2 -> 0; matrix products, arithmetic and copies ran while one was open for 2% -> 0% of each run, Pallas kernels for 0% -> 0%
where the time goes in v1:
time: 91.9 us; the launch traced here: 91.8 us
  Pallas kernels  85.7 us (93%)
  local copies, waits for them, and re-layouts  6.02 us (7%)
    pallas_call x1, Pallas kernels, on_device(): pl.pallas_call(kernel, out_shape=jax.ShapeDtypeStruct((KEEP, SLOTS, 2, DE...  85.7 us
    unnamed x1, local copies, waits for them, and re-layouts  6.02 us

profile of v1, /device:TPU:1, one launch (start us, length us, event | category | flops | bytes accessed | tf_op | source)
XLA Modules:
  0.0 91.8 jit_solution(5197185606654477992)
XLA Ops:
  0.0 85.7 %shard_map.55 = bf16[64,16,2,512]{3,2,1,0:T(2,128)(2,1)} custom-call(bf16[512,16,128]{2,1,0:T(8,128)(2,1)} %grid_hbm.1, bf16[16,512,512]{2,1,0:T(8,128)(2,1)} %leg_hbm.1, s32[512]{0:T(512)} %len_s.1, s32[512]{0:T(512)} %lat_s.1, s32[512]{0:T(512)} %wave_s.1, s32[4,128]{1,0:T(4,128)} %bitcast.2, s32[4,128]{1,0:T(4,128)} %bitcast.3), custom_call_target="tpu_custom_call" | custom-call | flops 14000000000 | bytes 14680064 | tf_op jit(solution)/shard_map/pallas_call | solution.py:293
  85.8 6.0 %copy.7 = bf16[64,16,2,512]{3,2,1,0:T(2,128)(2,1)} copy(bf16[64,16,2,512]{3,2,1,0:T(2,128)(2,1)} %shard_map.55) | data formatting | bytes 4194304

commit v2 on v1

v2 whole, which is shorter than its diff:
```python
import jax
import jax.numpy as jnp
from jax import lax
from jax.experimental import pallas as pl
from jax.experimental.pallas import tpu as pltpu
from jax.sharding import PartitionSpec as P

MESH = pl.DeviceIdType.MESH
BF16 = jnp.bfloat16
F32 = jnp.float32

LEVS = 8
WAVES = 32
ROWS = 16
SLOTS = 16
KEEP = 64
NLAT = 512
DEG = 512
NWAVE = 512
LANES = 128

CHUNKS = (4, 4, 4, 2, 1, 1)
STARTS = tuple(sum(CHUNKS[:i]) for i in range(len(CHUNKS)))
LAST = len(CHUNKS) - 1
CUT = WAVES * STARTS[LAST]
ZORDER = (4, 3, 5, 2, 6, 1, 7)

SIN_C = (3.14159264, -5.16771008, 2.55007752, -0.59829129, 0.07765766)
COS_C = (0.99999995, -4.93479283, 4.05841135, -1.33187657, 0.21968961)


def iota(shape, dim):
    return lax.broadcasted_iota(jnp.int32, shape, dim)


def horner(coefs, u):
    acc = u * coefs[-1] + coefs[-2]
    for c in coefs[-3::-1]:
        acc = acc * u + c
    return acc


def turn(count, width, inverse):
    whole = jnp.floor(count * inverse + 0.5)
    t = (count - whole * width) * inverse
    u = t * t
    s = t * horner(SIN_C, u)
    c = horner(COS_C, u)
    s2 = s + s
    return 1.0 - s2 * s, s2 * c


def nt_dot(a, b):
    return lax.dot_general(a, b, (((1,), (1,)), ((), ())), preferred_element_type=F32)


def dot(a, b):
    return jnp.dot(a, b, preferred_element_type=F32)


def set_swap(swap):
    i = iota((256, 256), 0)
    j = iota((256, 256), 1)
    swap[...] = jnp.where(j == (i % 16) * 16 + i // 16, 1.0, 0.0).astype(BF16)


def part_last():
    i = iota((LANES, LANES), 0)
    j = iota((LANES, LANES), 1)
    return jnp.where(j == (i % 2) * KEEP + i // 2, 1.0, 0.0).astype(BF16)


def kernel(grid_hbm, leg_hbm, len_s, lat_s, wave_s, lat_v, wave_v, acc, lp_last, fr_last,
           gin, g, x, table, turns, both, fs, fr, a, lraw, lp, onehot, swap, mcol,
           gin_sem, leg_sem, zs, zr, ws, wr):
    z = lax.axis_index("lev")
    w = lax.axis_index("wave")
    bar = pltpu.get_barrier_semaphore()

    def signal_z(i, carry):
        pl.semaphore_signal(bar, inc=1, device_id=(lax.rem(z + i, LEVS), w), device_id_type=MESH)
        return carry

    def signal_w(i, carry):
        pl.semaphore_signal(bar, inc=1, device_id=(z, lax.rem(w + i, WAVES)), device_id_type=MESH)
        return carry

    lax.fori_loop(1, LEVS, signal_z, 0)
    lax.fori_loop(1, WAVES, signal_w, 0)
    visit = ZORDER + (0,)

    def grid_copy(i):
        part = pl.ds(lax.rem(z + visit[i], LEVS) * KEEP, KEEP)
        return pltpu.make_async_copy(grid_hbm.at[part], gin.at[part], gin_sem.at[i])

    for i in range(LEVS):
        grid_copy(i).start()
    leg_copy = pltpu.make_async_copy(leg_hbm, lraw, leg_sem)
    leg_copy.start()

    set_swap(swap)

    def send_z(c, p):
        rows = CHUNKS[c]
        base = LEVS * STARTS[c]
        pltpu.make_async_remote_copy(
            src_ref=g.at[pl.ds(base + p * rows, rows)],
            dst_ref=x.at[pl.ds(base + z * rows, rows)],
            send_sem=zs.at[c], recv_sem=zr.at[c],
            device_id=(p, w), device_id_type=MESH,
        ).start()

    for i in range(LEVS):
        grid_copy(i).wait()
        p = lax.rem(z + visit[i], LEVS)
        for pair in range(2):
            k0 = pl.multiple_of(p * KEEP + pair * 32, 32)
            v = jnp.concatenate([gin[pl.ds(k0 + 16 * h, 16)].reshape(256, LANES) for h in range(2)], axis=1)
            v = dot(swap[...], v).astype(BF16)
            for h in range(2):
                kk = pair * 32 + 16 * h
                part = v[:, LANES * h : LANES * (h + 1)].reshape(16, 16, LANES)
                for c, rows in enumerate(CHUNKS):
                    r0 = STARTS[c]
                    dest = g if i < LEVS - 1 else x
                    dest[pl.ds(LEVS * r0 + p * rows, rows), kk : kk + 16, :] = part[r0 : r0 + rows]
        if i == 0:
            pl.semaphore_wait(bar, LEVS - 1 + WAVES - 1)
        if i < LEVS - 1:
            send_z(0, p)
    for c in range(1, len(CHUNKS)):
        for o in ZORDER:
            send_z(c, lax.rem(z + o, LEVS))

    col = jnp.zeros((NWAVE, LANES), F32)
    for t in range(4):
        hit = iota((NWAVE, LANES), 1) + LANES * t == iota((NWAVE, LANES), 0)
        col = col + jnp.where(hit, wave_v[t : t + 1, :].astype(F32), 0.0)
    mcol[...] = jnp.broadcast_to(jnp.sum(col, axis=1, keepdims=True), (NWAVE, LANES))
    for c, rows in enumerate(CHUNKS):
        n = WAVES * rows
        q = iota((n, LANES), 0)
        row = (q // rows) * ROWS + STARTS[c] + q % rows
        col = jnp.zeros((n, LANES), F32)
        for t in range(4):
            hit = iota((n, LANES), 1) + LANES * t == row
            col = col + jnp.where(hit, lat_v[t : t + 1, :].astype(F32), 0.0)
        lat = jnp.sum(col, axis=1, keepdims=True)
        onehot[WAVES * STARTS[c] : WAVES * STARTS[c] + n, :] = jnp.where(
            iota((n, NLAT), 1).astype(F32) == lat, 1.0, 0.0
        ).astype(BF16)

    def make_table(r0, rows):
        def one(rr, carry):
            length = len_s[lat_s[w * ROWS + r0 + rr]]
            width = jnp.full((1, LANES), length, jnp.int32).astype(F32)
            inverse = 1.0 / width
            factor = 1.0 / jnp.sqrt(width)
            lane = iota((32, LANES), 1)
            left = lane < KEEP
            low = lane.astype(F32)

            def block(b, carry2):
                s0 = pl.multiple_of(b * 32, 32)
                rows_c = pl.ds(s0, 32)
                rows_s = pl.ds(NWAVE + s0, 32)
                m = mcol[rows_c, :]
                cl, sl = turn(m * low, width, inverse)
                table[rr, rows_c, :LANES] = cl.astype(BF16)
                table[rr, rows_s, :LANES] = sl.astype(BF16)
                c1, s1 = turn(m * float(LANES), width, inverse)
                table[rr, rows_c, LANES:] = (cl * c1 - sl * s1).astype(BF16)
                table[rr, rows_s, LANES:] = (sl * c1 + cl * s1).astype(BF16)
                t = s1 + s1
                c2, s2 = 1.0 - t * s1, t * c1
                t = s2 + s2
                c4, s4 = factor - t * (s2 * factor), t * (c2 * factor)
                turns[rr, rows_c, :LANES] = jnp.where(left, 1.0, c2) * factor
                turns[rr, rows_s, :LANES] = jnp.where(left, 0.0, s2) * factor
                turns[rr, rows_c, LANES:] = jnp.where(left, c4, c4 * c2 - s4 * s2)
                turns[rr, rows_s, LANES:] = jnp.where(left, s4, s4 * c2 + c4 * s2)
                return carry2

            lax.fori_loop(0, NWAVE // 32, block, 0, unroll=2)
            return carry

        lax.fori_loop(0, rows, one, 0)

    def transform(r0, rows):
        left = iota((32, LANES), 1) < KEEP

        def one(rr, carry):
            length = len_s[lat_s[w * ROWS + r0 + rr]]
            parts = []
            for d in range(LEVS):
                inside = iota((KEEP, LANES), 1) + d * LANES < length
                keep = jnp.where(inside, 1.0, 0.0).astype(BF16)
                parts.append(x[LEVS * r0 + d * rows + rr] * keep)
            lines = jnp.concatenate(
                [jnp.concatenate(parts[2 * d : 2 * d + 2], axis=1) for d in range(4)], axis=0
            )
            both[...] = nt_dot(table[rr], lines)
            for b in range(NWAVE // 32):
                rows_c = slice(32 * b, 32 * (b + 1))
                rows_s = slice(NWAVE + 32 * b, NWAVE + 32 * (b + 1))
                real, imag = 0.0, 0.0
                for t in range(2):
                    cols = slice(LANES * t, LANES * (t + 1))
                    u, v = both[rows_c, cols], both[rows_s, cols]
                    c, q = turns[rr, rows_c, cols], turns[rr, rows_s, cols]
                    real = real + (c * u - q * v)
                    imag = imag - (q * u + c * v)
                f = jnp.where(left, real, pltpu.roll(imag, KEEP, axis=1))
                f = f + jnp.where(left, pltpu.roll(real, KEEP, axis=1), imag)
                f = f.astype(BF16)
                for i in range(2):
                    fs[WAVES * r0 + (2 * b + i) * rows + rr] = f[SLOTS * i : SLOTS * (i + 1)]
            return carry

        lax.fori_loop(0, rows, one, 0)

    def landing(c, first, count):
        if c == LAST:
            return fr_last.at[pl.ds(first, count)]
        return fr.at[pl.ds(WAVES * STARTS[c] + first, count)]

    def send_wave(c):
        rows = CHUNKS[c]
        base = WAVES * STARTS[c]

        def one(o, carry):
            px = lax.rem(w // 8 + o // 8, 4)
            py = lax.rem(lax.rem(w // 2, 4) + lax.rem(o // 2, 4), 4)
            pc = lax.rem(lax.rem(w, 2) + lax.rem(o, 2), 2)
            p = px * 8 + py * 2 + pc
            pltpu.make_async_remote_copy(
                src_ref=fs.at[pl.ds(base + p * rows, rows)],
                dst_ref=landing(c, w * rows, rows),
                send_sem=ws.at[c], recv_sem=wr.at[c],
                device_id=(z, p), device_id_type=MESH,
            ).start()
            return carry

        lax.fori_loop(1, WAVES, one, 0)
        own = pl.ds(base + w * rows, rows)
        if c == LAST:
            fr_last[pl.ds(w * rows, rows)] = fs[own]
        else:
            fr[own] = fs[own]

    def z_all(c):
        region = pl.ds(LEVS * STARTS[c], (LEVS - 1) * CHUNKS[c])
        return pltpu.make_async_remote_copy(
            src_ref=g.at[region], dst_ref=x.at[region], send_sem=zs.at[c], recv_sem=zr.at[c],
            device_id=(lax.rem(z + 1, LEVS), w), device_id_type=MESH)

    def wave_all(c):
        region = pl.ds(WAVES * STARTS[c], (WAVES - 1) * CHUNKS[c])
        return pltpu.make_async_remote_copy(
            src_ref=fs.at[region], dst_ref=landing(c, 0, (WAVES - 1) * CHUNKS[c]),
            send_sem=ws.at[c], recv_sem=wr.at[c],
            device_id=(z, lax.rem(w + 1, WAVES)), device_id_type=MESH)

    def to_slots(c):
        first = WAVES * STARTS[c] // 32

        def one(b, carry):
            q = pl.multiple_of(b * 32, 32)
            v = jnp.concatenate([fr[pl.ds(q + 16 * h, 16)].reshape(256, LANES) for h in range(2)], axis=1)
            v = dot(swap[...], v).astype(BF16)
            for h in range(2):
                a[:, pl.ds(q + 16 * h, 16), :] = v[:, LANES * h : LANES * (h + 1)].reshape(16, 16, LANES)
            return carry

        lax.fori_loop(first, first + CHUNKS[c], one, 0, unroll=2)

    make_table(0, CHUNKS[0])

    leg_copy.wait()

    def order_legendre(s, carry):
        m = wave_s[w * SLOTS + s]
        for h in range(2):
            cols = slice(256 * h, 256 * (h + 1))
            keep = iota((256, 256), 1) + 256 * h >= m
            for q in range(2):
                rows = slice(256 * q, 256 * (q + 1))
                v = dot(onehot[rows, :], lraw[s, :, cols])
                lp[s, rows, cols] = jnp.where(keep, v, 0.0).astype(BF16)
        return carry

    lax.fori_loop(0, SLOTS, order_legendre, 0)

    lp_last[...] = lp[:, CUT:, :]

    for c in range(len(CHUNKS)):
        z_all(c).wait_recv()
        transform(STARTS[c], CHUNKS[c])
        send_wave(c)
        if c < LAST:
            make_table(STARTS[c + 1], CHUNKS[c + 1])
        if c > 0:
            wave_all(c - 1).wait_recv()
            to_slots(c - 1)

    order = part_last()

    def sum_first(s, carry):
        at = nt_dot(order, a[s, :, :]).astype(BF16)
        acc[s] = dot(at, lp[s, :CUT, :])
        return carry

    lax.fori_loop(0, SLOTS, sum_first, 0, unroll=4)

    wave_all(LAST).wait_recv()

    for c in range(len(CHUNKS)):
        z_all(c).wait_send()
        wave_all(c).wait_send()


def finish(acc, lp, fr, out_ref, a, swap):
    tail = NLAT - CUT
    group = out_ref.shape[1]

    @pl.when(pl.program_id(0) == 0)
    def _():
        set_swap(swap)
        for b in range(tail // 32):
            v = jnp.concatenate([fr[32 * b + 16 * h : 32 * b + 16 * h + 16].reshape(256, LANES) for h in range(2)], axis=1)
            v = dot(swap[...], v).astype(BF16)
            for h in range(2):
                q = 32 * b + 16 * h
                a[:, q : q + 16, :] = v[:, LANES * h : LANES * (h + 1)].reshape(16, 16, LANES)

    first = pl.multiple_of(pl.program_id(0) * group, group)
    slots = pl.ds(first, group)
    at = nt_dot(part_last(), a[slots].reshape(group * tail, LANES)).astype(BF16)
    weights = lp[slots].reshape(group * tail, DEG)
    slot = iota((LANES, group * tail), 1) // tail
    for s in range(group):
        own = jnp.where(slot == s, 1.0, 0.0).astype(BF16)
        total = acc[first + s] + dot(at * own, weights)
        out_ref[:, s] = total.astype(BF16).reshape(KEEP, 2, DEG)


def on_device(grid, legendre, lengths, lat_order, wave_order):
    any_spec = pl.BlockSpec(memory_space=pl.ANY)
    smem = pl.BlockSpec(memory_space=pltpu.SMEM)
    vmem = pl.BlockSpec(memory_space=pltpu.VMEM)
    n = len(CHUNKS)
    dma = pltpu.SemaphoreType.DMA
    tail = NLAT - CUT
    group = 4
    acc, lp, fr = pl.pallas_call(
        kernel,
        out_shape=[
            pltpu.VMEM((SLOTS, 2 * KEEP, DEG), F32),
            pltpu.VMEM((SLOTS, tail, DEG), BF16),
            pltpu.VMEM((tail, SLOTS, LANES), BF16),
        ],
        in_specs=[any_spec, any_spec, smem, smem, smem, vmem, vmem],
        out_specs=[vmem] * 3,
        scratch_shapes=[
            pltpu.VMEM((512, ROWS, LANES), BF16),
            pltpu.VMEM((LEVS * ROWS, KEEP, LANES), BF16),
            pltpu.VMEM((LEVS * ROWS, KEEP, LANES), BF16),
            pltpu.VMEM((max(CHUNKS), 2 * NWAVE, 2 * LANES), BF16),
            pltpu.VMEM((max(CHUNKS), 2 * NWAVE, 2 * LANES), F32),
            pltpu.VMEM((2 * NWAVE, 2 * LANES), F32),
            pltpu.VMEM((WAVES * ROWS, SLOTS, LANES), BF16),
            pltpu.VMEM((CUT, SLOTS, LANES), BF16),
            pltpu.VMEM((SLOTS, CUT, LANES), BF16),
            pltpu.VMEM((SLOTS, NLAT, DEG), BF16),
            pltpu.VMEM((SLOTS, NLAT, DEG), BF16),
            pltpu.VMEM((NLAT, NLAT), BF16),
            pltpu.VMEM((256, 256), BF16),
            pltpu.VMEM((NWAVE, LANES), F32),
            dma((LEVS,)), dma, dma((n,)), dma((n,)), dma((n,)), dma((n,)),
        ],
        compiler_params=pltpu.CompilerParams(
            collective_id=0, has_side_effects=True, vmem_limit_bytes=55 << 20
        ),
        cost_estimate=pl.CostEstimate(flops=14 * 10**9, bytes_accessed=14 << 20, transcendentals=0),
    )(grid, legendre, lengths, lat_order, wave_order, lat_order.reshape(4, 128), wave_order.reshape(4, 128))
    return pl.pallas_call(
        finish,
        grid=(SLOTS // group,),
        out_shape=jax.ShapeDtypeStruct((KEEP, SLOTS, 2, DEG), BF16),
        in_specs=[vmem] * 3,
        out_specs=pl.BlockSpec((KEEP, group, 2, DEG), lambda i: (0, i, 0, 0)),
        scratch_shapes=[pltpu.VMEM((SLOTS, tail, LANES), BF16), pltpu.VMEM((256, 256), BF16)],
        compiler_params=pltpu.CompilerParams(vmem_limit_bytes=32 << 20),
    )(acc, lp, fr)


def solution(mesh):
    return jax.shard_map(
        on_device,
        mesh=mesh,
        in_specs=(P(None, "wave", "lev"), P("wave", None, None), P(), P(), P()),
        out_specs=P("lev", "wave", None, None),
        check_vma=False,
    )
```

time: 91.9 us -> 76 us (0.83)
  Pallas kernels: 85.7 us -> 75.9 us
  local copies, waits for them, and re-layouts: 6.02 us -> 0 us
    pallas_call x1 -> x2, Pallas kernels: 85.7 us -> 75.9 us  [the longest x1 72.7 us: on_device(): pl.pallas_call(kernel, out_shape=[pltpu.VMEM((SLOTS, 2 * KEEP, DEG), F32)...]
    unnamed x1 -> x0, local copies, waits for them, and re-layouts: 6.02 us -> none
where the time goes in v2:
time: 76 us; the launch traced here: 75.9 us
  Pallas kernels  75.9 us (100%)
    pallas_call x1, Pallas kernels, on_device(): pl.pallas_call(kernel, out_shape=[pltpu.VMEM((SLOTS, 2 * KEEP, DEG), F32)...  72.7 us
    pallas_call x1, Pallas kernels, on_device(): pl.pallas_call(finish, grid=(SLOTS // group,), out_shape=jax.ShapeDtypeSt...  3.18 us

profile of v2, /device:TPU:1, one launch (start us, length us, event | category | flops | bytes accessed | tf_op | source)
XLA Modules:
  0.0 75.9 jit_solution(4456980763819381639)
XLA Ops:
  0.0 72.7 %shard_map.55 = (f32[16,128,512]{2,1,0:T(8,128)S(1)}, bf16[16,32,512]{2,1,0:T(8,128)(2,1)S(1)}, bf16[32,16,128]{2,1,0:T(8,128)(2,1)S(1)}) custom-call(bf16[512,16,128]{2,1,0:T(8,128)(2,1)} %grid_hbm.1, bf16[16,512,512]{2,1,0:T(8,128)(2,1)} %leg_hbm.1, s32[512]{0:T(512)} %len_s.1, s32[512]{0:T(512)} %lat_s.1, s32[512]{0:T(512)} %wave_s.1, s32[4,128]{1,0:T(4,128)} %bitcast.2, ...), custom_call_target="tpu_custom_call" | custom-call | flops 14000000000 | bytes 14680064 | tf_op jit(solution)/shard_map/pallas_call | solution.py:355
  72.7 3.2 %shard_map.56 = bf16[64,16,2,512]{3,2,1,0:T(2,128)(2,1)} custom-call(f32[16,128,512]{2,1,0:T(8,128)S(1)} %get-tuple-element.8.acc, bf16[16,32,512]{2,1,0:T(8,128)(2,1)S(1)} %get-tuple-element.9.lp, bf16[32,16,128]{2,1,0:T(8,128)(2,1)S(1)} %get-tuple-element.10.fr), custom_call_target="tpu_custom_call" | custom-call | tf_op jit(solution)/shard_map/pallas_call | solution.py:386

commit v3 on v2

--- a/solution.py
+++ b/solution.py
@@ -23,6 +23,8 @@
 STARTS = tuple(sum(CHUNKS[:i]) for i in range(len(CHUNKS)))
 LAST = len(CHUNKS) - 1
 CUT = WAVES * STARTS[LAST]
+HEAD = 256
+TABLES = 8
 ZORDER = (4, 3, 5, 2, 6, 1, 7)
 
 SIN_C = (3.14159264, -5.16771008, 2.55007752, -0.59829129, 0.07765766)
@@ -70,8 +72,8 @@
     return jnp.where(j == (i % 2) * KEEP + i // 2, 1.0, 0.0).astype(BF16)
 
 
-def kernel(grid_hbm, leg_hbm, len_s, lat_s, wave_s, lat_v, wave_v, acc, lp_last, fr_last,
-           gin, g, x, table, turns, both, fs, fr, a, lraw, lp, onehot, swap, mcol,
+def kernel(grid_hbm, leg_hbm, len_s, lat_s, wave_s, lat_v, wave_v, acc, lp_tail, a_tail, fr_last,
+           gin, g, x, table, turns, both, fs, fr, a_head, lraw, lp_head, onehot, swap, mcol,
            gin_sem, leg_sem, zs, zr, ws, wr):
     z = lax.axis_index("lev")
     w = lax.axis_index("wave")
@@ -152,6 +154,7 @@
 
     def make_table(r0, rows):
         def one(rr, carry):
+            held = r0 % TABLES + rr
             length = len_s[lat_s[w * ROWS + r0 + rr]]
             width = jnp.full((1, LANES), length, jnp.int32).astype(F32)
             inverse = 1.0 / width
@@ -166,19 +169,19 @@
                 rows_s = pl.ds(NWAVE + s0, 32)
                 m = mcol[rows_c, :]
                 cl, sl = turn(m * low, width, inverse)
-                table[rr, rows_c, :LANES] = cl.astype(BF16)
-                table[rr, rows_s, :LANES] = sl.astype(BF16)
+                table[held, rows_c, :LANES] = cl.astype(BF16)
+                table[held, rows_s, :LANES] = sl.astype(BF16)
                 c1, s1 = turn(m * float(LANES), width, inverse)
-                table[rr, rows_c, LANES:] = (cl * c1 - sl * s1).astype(BF16)
-                table[rr, rows_s, LANES:] = (sl * c1 + cl * s1).astype(BF16)
+                table[held, rows_c, LANES:] = (cl * c1 - sl * s1).astype(BF16)
+                table[held, rows_s, LANES:] = (sl * c1 + cl * s1).astype(BF16)
                 t = s1 + s1
                 c2, s2 = 1.0 - t * s1, t * c1
                 t = s2 + s2
                 c4, s4 = factor - t * (s2 * factor), t * (c2 * factor)
-                turns[rr, rows_c, :LANES] = jnp.where(left, 1.0, c2) * factor
-                turns[rr, rows_s, :LANES] = jnp.where(left, 0.0, s2) * factor
-                turns[rr, rows_c, LANES:] = jnp.where(left, c4, c4 * c2 - s4 * s2)
-                turns[rr, rows_s, LANES:] = jnp.where(left, s4, s4 * c2 + c4 * s2)
+                turns[held, rows_c, :LANES] = jnp.where(left, 1.0, c2) * factor
+                turns[held, rows_s, :LANES] = jnp.where(left, 0.0, s2) * factor
+                turns[held, rows_c, LANES:] = jnp.where(left, c4, c4 * c2 - s4 * s2)
+                turns[held, rows_s, LANES:] = jnp.where(left, s4, s4 * c2 + c4 * s2)
                 return carry2
 
             lax.fori_loop(0, NWAVE // 32, block, 0, unroll=2)
@@ -191,6 +194,7 @@
 
         def one(rr, carry):
             length = len_s[lat_s[w * ROWS + r0 + rr]]
+            held = r0 % TABLES + rr
             parts = []
             for d in range(LEVS):
                 inside = iota((KEEP, LANES), 1) + d * LANES < length
@@ -199,7 +203,7 @@
             lines = jnp.concatenate(
                 [jnp.concatenate(parts[2 * d : 2 * d + 2], axis=1) for d in range(4)], axis=0
             )
-            both[...] = nt_dot(table[rr], lines)
+            both[...] = nt_dot(table[held], lines)
             for b in range(NWAVE // 32):
                 rows_c = slice(32 * b, 32 * (b + 1))
                 rows_s = slice(NWAVE + 32 * b, NWAVE + 32 * (b + 1))
@@ -207,7 +211,7 @@
                 for t in range(2):
                     cols = slice(LANES * t, LANES * (t + 1))
                     u, v = both[rows_c, cols], both[rows_s, cols]
-                    c, q = turns[rr, rows_c, cols], turns[rr, rows_s, cols]
+                    c, q = turns[held, rows_c, cols], turns[held, rows_s, cols]
                     real = real + (c * u - q * v)
                     imag = imag - (q * u + c * v)
                 f = jnp.where(left, real, pltpu.roll(imag, KEEP, axis=1))
@@ -262,17 +266,19 @@
             device_id=(z, lax.rem(w + 1, WAVES)), device_id_type=MESH)
 
     def to_slots(c):
-        first = WAVES * STARTS[c] // 32
+        begin = WAVES * STARTS[c]
+        dest, skip = (a_head, 0) if begin < HEAD else (a_tail, HEAD)
 
         def one(b, carry):
             q = pl.multiple_of(b * 32, 32)
             v = jnp.concatenate([fr[pl.ds(q + 16 * h, 16)].reshape(256, LANES) for h in range(2)], axis=1)
             v = dot(swap[...], v).astype(BF16)
             for h in range(2):
-                a[:, pl.ds(q + 16 * h, 16), :] = v[:, LANES * h : LANES * (h + 1)].reshape(16, 16, LANES)
+                to = pl.ds(q - skip + 16 * h, 16)
+                dest[:, to, :] = v[:, LANES * h : LANES * (h + 1)].reshape(16, 16, LANES)
             return carry
 
-        lax.fori_loop(first, first + CHUNKS[c], one, 0, unroll=2)
+        lax.fori_loop(begin // 32, begin // 32 + CHUNKS[c], one, 0, unroll=min(2, CHUNKS[c]))
 
     make_table(0, CHUNKS[0])
 
@@ -286,32 +292,43 @@
             for q in range(2):
                 rows = slice(256 * q, 256 * (q + 1))
                 v = dot(onehot[rows, :], lraw[s, :, cols])
-                lp[s, rows, cols] = jnp.where(keep, v, 0.0).astype(BF16)
+                part = lp_head if q == 0 else lp_tail
+                part[s, :, cols] = jnp.where(keep, v, 0.0).astype(BF16)
         return carry
 
     lax.fori_loop(0, SLOTS, order_legendre, 0)
 
-    lp_last[...] = lp[:, CUT:, :]
-
-    for c in range(len(CHUNKS)):
+    def arrive(c):
         z_all(c).wait_recv()
         transform(STARTS[c], CHUNKS[c])
         send_wave(c)
-        if c < LAST:
-            make_table(STARTS[c + 1], CHUNKS[c + 1])
-        if c > 0:
-            wave_all(c - 1).wait_recv()
-            to_slots(c - 1)
+
+    def collect(c):
+        wave_all(c).wait_recv()
+        to_slots(c)
+
+    make_table(STARTS[1], CHUNKS[1])
+    arrive(0)
+    make_table(STARTS[2], CHUNKS[2])
+    arrive(1)
+    make_table(STARTS[3], ROWS - STARTS[3])
+    collect(0)
+    arrive(2)
+    collect(1)
 
     order = part_last()
 
     def sum_first(s, carry):
-        at = nt_dot(order, a[s, :, :]).astype(BF16)
-        acc[s] = dot(at, lp[s, :CUT, :])
+        at = nt_dot(order, a_head[s]).astype(BF16)
+        acc[s] = dot(at, lp_head[s])
         return carry
 
     lax.fori_loop(0, SLOTS, sum_first, 0, unroll=4)
 
+    for c in range(3, LAST + 1):
+        arrive(c)
+    for c in range(2, LAST):
+        collect(c)
     wave_all(LAST).wait_recv()
 
     for c in range(len(CHUNKS)):
@@ -319,28 +336,24 @@
         wave_all(c).wait_send()
 
 
-def finish(acc, lp, fr, out_ref, a, swap):
-    tail = NLAT - CUT
+def finish(acc, lp_tail, a_tail, fr, out_ref, a, swap):
     group = out_ref.shape[1]
+    tail = NLAT - HEAD
+    ready = CUT - HEAD
 
     @pl.when(pl.program_id(0) == 0)
     def _():
         set_swap(swap)
-        for b in range(tail // 32):
-            v = jnp.concatenate([fr[32 * b + 16 * h : 32 * b + 16 * h + 16].reshape(256, LANES) for h in range(2)], axis=1)
-            v = dot(swap[...], v).astype(BF16)
-            for h in range(2):
-                q = 32 * b + 16 * h
-                a[:, q : q + 16, :] = v[:, LANES * h : LANES * (h + 1)].reshape(16, 16, LANES)
+        v = jnp.concatenate([fr[16 * h : 16 * h + 16].reshape(256, LANES) for h in range(2)], axis=1)
+        v = dot(swap[...], v).astype(BF16)
+        for h in range(2):
+            a[:, ready + 16 * h : ready + 16 * h + 16, :] = v[:, LANES * h : LANES * (h + 1)].reshape(16, 16, LANES)
+        a[:, :ready, :] = a_tail[...]
 
     first = pl.multiple_of(pl.program_id(0) * group, group)
-    slots = pl.ds(first, group)
-    at = nt_dot(part_last(), a[slots].reshape(group * tail, LANES)).astype(BF16)
-    weights = lp[slots].reshape(group * tail, DEG)
-    slot = iota((LANES, group * tail), 1) // tail
+    at = nt_dot(part_last(), a[pl.ds(first, group)].reshape(group * tail, LANES)).astype(BF16)
     for s in range(group):
-        own = jnp.where(slot == s, 1.0, 0.0).astype(BF16)
-        total = acc[first + s] + dot(at * own, weights)
+        total = acc[first + s] + dot(at[:, tail * s : tail * (s + 1)], lp_tail[first + s])
         out_ref[:, s] = total.astype(BF16).reshape(KEEP, 2, DEG)
 
 
@@ -350,36 +363,36 @@
     vmem = pl.BlockSpec(memory_space=pltpu.VMEM)
     n = len(CHUNKS)
     dma = pltpu.SemaphoreType.DMA
-    tail = NLAT - CUT
     group = 4
-    acc, lp, fr = pl.pallas_call(
+    parts = pl.pallas_call(
         kernel,
         out_shape=[
             pltpu.VMEM((SLOTS, 2 * KEEP, DEG), F32),
-            pltpu.VMEM((SLOTS, tail, DEG), BF16),
-            pltpu.VMEM((tail, SLOTS, LANES), BF16),
+            pltpu.VMEM((SLOTS, NLAT - HEAD, DEG), BF16),
+            pltpu.VMEM((SLOTS, CUT - HEAD, LANES), BF16),
+            pltpu.VMEM((NLAT - CUT, SLOTS, LANES), BF16),
         ],
         in_specs=[any_spec, any_spec, smem, smem, smem, vmem, vmem],
-        out_specs=[vmem] * 3,
+        out_specs=[vmem] * 4,
         scratch_shapes=[
             pltpu.VMEM((512, ROWS, LANES), BF16),
             pltpu.VMEM((LEVS * ROWS, KEEP, LANES), BF16),
             pltpu.VMEM((LEVS * ROWS, KEEP, LANES), BF16),
-            pltpu.VMEM((max(CHUNKS), 2 * NWAVE, 2 * LANES), BF16),
-            pltpu.VMEM((max(CHUNKS), 2 * NWAVE, 2 * LANES), F32),
+            pltpu.VMEM((TABLES, 2 * NWAVE, 2 * LANES), BF16),
+            pltpu.VMEM((TABLES, 2 * NWAVE, 2 * LANES), F32),
             pltpu.VMEM((2 * NWAVE, 2 * LANES), F32),
             pltpu.VMEM((WAVES * ROWS, SLOTS, LANES), BF16),
             pltpu.VMEM((CUT, SLOTS, LANES), BF16),
-            pltpu.VMEM((SLOTS, CUT, LANES), BF16),
+            pltpu.VMEM((SLOTS, HEAD, LANES), BF16),
             pltpu.VMEM((SLOTS, NLAT, DEG), BF16),
-            pltpu.VMEM((SLOTS, NLAT, DEG), BF16),
+            pltpu.VMEM((SLOTS, HEAD, DEG), BF16),
             pltpu.VMEM((NLAT, NLAT), BF16),
             pltpu.VMEM((256, 256), BF16),
             pltpu.VMEM((NWAVE, LANES), F32),
             dma((LEVS,)), dma, dma((n,)), dma((n,)), dma((n,)), dma((n,)),
         ],
         compiler_params=pltpu.CompilerParams(
-            collective_id=0, has_side_effects=True, vmem_limit_bytes=55 << 20
+            collective_id=0, has_side_effects=True, vmem_limit_bytes=51 << 20
         ),
         cost_estimate=pl.CostEstimate(flops=14 * 10**9, bytes_accessed=14 << 20, transcendentals=0),
     )(grid, legendre, lengths, lat_order, wave_order, lat_order.reshape(4, 128), wave_order.reshape(4, 128))
@@ -387,11 +400,11 @@
         finish,
         grid=(SLOTS // group,),
         out_shape=jax.ShapeDtypeStruct((KEEP, SLOTS, 2, DEG), BF16),
-        in_specs=[vmem] * 3,
+        in_specs=[vmem] * 4,
         out_specs=pl.BlockSpec((KEEP, group, 2, DEG), lambda i: (0, i, 0, 0)),
-        scratch_shapes=[pltpu.VMEM((SLOTS, tail, LANES), BF16), pltpu.VMEM((256, 256), BF16)],
+        scratch_shapes=[pltpu.VMEM((SLOTS, NLAT - HEAD, LANES), BF16), pltpu.VMEM((256, 256), BF16)],
         compiler_params=pltpu.CompilerParams(vmem_limit_bytes=32 << 20),
-    )(acc, lp, fr)
+    )(*parts)
 
 
 def solution(mesh):

time: 76 us -> 68.6 us (0.903)
  Pallas kernels: 75.9 us -> 68.5 us
    pallas_call x1, Pallas kernels: 72.7 us -> 65.4 us  [on_device(): pl.pallas_call(kernel, out_shape=[pltpu.VMEM((SLOTS, 2 * KEEP, DEG), F32)...]
where the time goes in v3:
time: 68.6 us; the launch traced here: 68.5 us
  Pallas kernels  68.5 us (100%)
    pallas_call x1, Pallas kernels, on_device(): pl.pallas_call(kernel, out_shape=[pltpu.VMEM((SLOTS, 2 * KEEP, DEG), F32)...  65.4 us
    pallas_call x1, Pallas kernels, on_device(): pl.pallas_call(finish, grid=(SLOTS // group,), out_shape=jax.ShapeDtypeSt...  3.16 us

profile of v3, /device:TPU:1, one launch (start us, length us, event | category | flops | bytes accessed | tf_op | source)
XLA Modules:
  0.0 68.5 jit_solution(10132796174828096432)
XLA Ops:
  0.0 65.4 %shard_map.55 = (f32[16,128,512]{2,1,0:T(8,128)S(1)}, bf16[16,256,512]{2,1,0:T(8,128)(2,1)S(1)}, bf16[16,224,128]{2,1,0:T(8,128)(2,1)S(1)}, bf16[32,16,128]{2,1,0:T(8,128)(2,1)S(1)}) custom-call(bf16[512,16,128]{2,1,0:T(8,128)(2,1)} %grid_hbm.1, bf16[16,512,512]{2,1,0:T(8,128)(2,1)} %leg_hbm.1, s32[512]{0:T(512)} %len_s.1, s32[512]{0:T(512)} %lat_s.1, ...), custom_call_target="tpu_custom_call" | custom-call | flops 14000000000 | bytes 14680064 | tf_op jit(solution)/shard_map/pallas_call | solution.py:367
  65.4 3.2 %shard_map.56 = bf16[64,16,2,512]{3,2,1,0:T(2,128)(2,1)} custom-call(f32[16,128,512]{2,1,0:T(8,128)S(1)} %get-tuple-element.9.acc, bf16[16,256,512]{2,1,0:T(8,128)(2,1)S(1)} %get-tuple-element.10.lp_tail, bf16[16,224,128]{2,1,0:T(8,128)(2,1)S(1)} %get-tuple-element.11.a_tail, bf16[32,16,128]{2,1,0:T(8,128)(2,1)S(1)} %get-tuple-element.12.fr), custom_call_target="tpu_custom_call" | custom-call | tf_op jit(solution)/shard_map/pallas_call | solution.py:399

commit v4 on v3

--- a/solution.py
+++ b/solution.py
@@ -63,18 +63,18 @@
 def set_swap(swap):
     i = iota((256, 256), 0)
     j = iota((256, 256), 1)
-    swap[...] = jnp.where(j == (i % 16) * 16 + i // 16, 1.0, 0.0).astype(BF16)
+    swap[...] = jnp.where(j == (i & 15) * 16 + (i >> 4), 1.0, 0.0).astype(BF16)
 
 
 def part_last():
     i = iota((LANES, LANES), 0)
     j = iota((LANES, LANES), 1)
-    return jnp.where(j == (i % 2) * KEEP + i // 2, 1.0, 0.0).astype(BF16)
-
-
-def kernel(grid_hbm, leg_hbm, len_s, lat_s, wave_s, lat_v, wave_v, acc, lp_tail, a_tail, fr_last,
+    return jnp.where(j == (i & 1) * KEEP + (i >> 1), 1.0, 0.0).astype(BF16)
+
+
+def kernel(grid_hbm, leg_hbm, len_hbm, lat_hbm, wave_hbm, lat4_hbm, wave4_hbm, acc, lp_tail, a_tail, fr_last,
            gin, g, x, table, turns, both, fs, fr, a_head, lraw, lp_head, onehot, swap, mcol,
-           gin_sem, leg_sem, zs, zr, ws, wr):
+           len_s, lat_s, wave_s, lat_v, wave_v, gin_sem, leg_sem, small_sem, zs, zr, ws, wr):
     z = lax.axis_index("lev")
     w = lax.axis_index("wave")
     bar = pltpu.get_barrier_semaphore()
@@ -87,8 +87,6 @@
         pl.semaphore_signal(bar, inc=1, device_id=(z, lax.rem(w + i, WAVES)), device_id_type=MESH)
         return carry
 
-    lax.fori_loop(1, LEVS, signal_z, 0)
-    lax.fori_loop(1, WAVES, signal_w, 0)
     visit = ZORDER + (0,)
 
     def grid_copy(i):
@@ -97,6 +95,16 @@
 
     for i in range(LEVS):
         grid_copy(i).start()
+    lax.fori_loop(1, LEVS, signal_z, 0)
+    lax.fori_loop(1, WAVES, signal_w, 0)
+    small = [
+        pltpu.make_async_copy(src, dst, small_sem.at[i])
+        for i, (src, dst) in enumerate(
+            [(len_hbm, len_s), (lat_hbm, lat_s), (wave_hbm, wave_s), (lat4_hbm, lat_v), (wave4_hbm, wave_v)]
+        )
+    ]
+    for copy in small:
+        copy.start()
     leg_copy = pltpu.make_async_copy(leg_hbm, lraw, leg_sem)
     leg_copy.start()
 
@@ -134,6 +142,8 @@
         for o in ZORDER:
             send_z(c, lax.rem(z + o, LEVS))
 
+    for copy in small:
+        copy.wait()
     col = jnp.zeros((NWAVE, LANES), F32)
     for t in range(4):
         hit = iota((NWAVE, LANES), 1) + LANES * t == iota((NWAVE, LANES), 0)
@@ -245,7 +255,7 @@
             ).start()
             return carry
 
-        lax.fori_loop(1, WAVES, one, 0)
+        lax.fori_loop(1, WAVES, one, 0, unroll=c == LAST)
         own = pl.ds(base + w * rows, rows)
         if c == LAST:
             fr_last[pl.ds(w * rows, rows)] = fs[own]
@@ -336,34 +346,35 @@
         wave_all(c).wait_send()
 
 
-def finish(acc, lp_tail, a_tail, fr, out_ref, a, swap):
-    group = out_ref.shape[1]
+def finish(acc, lp_tail, a_tail, fr, out_hbm, out, a, swap, sems):
+    group = 4
     tail = NLAT - HEAD
     ready = CUT - HEAD
-
-    @pl.when(pl.program_id(0) == 0)
-    def _():
-        set_swap(swap)
-        v = jnp.concatenate([fr[16 * h : 16 * h + 16].reshape(256, LANES) for h in range(2)], axis=1)
-        v = dot(swap[...], v).astype(BF16)
-        for h in range(2):
-            a[:, ready + 16 * h : ready + 16 * h + 16, :] = v[:, LANES * h : LANES * (h + 1)].reshape(16, 16, LANES)
-        a[:, :ready, :] = a_tail[...]
-
-    first = pl.multiple_of(pl.program_id(0) * group, group)
-    at = nt_dot(part_last(), a[pl.ds(first, group)].reshape(group * tail, LANES)).astype(BF16)
-    for s in range(group):
-        total = acc[first + s] + dot(at[:, tail * s : tail * (s + 1)], lp_tail[first + s])
-        out_ref[:, s] = total.astype(BF16).reshape(KEEP, 2, DEG)
+    set_swap(swap)
+    v = jnp.concatenate([fr[16 * h : 16 * h + 16].reshape(256, LANES) for h in range(2)], axis=1)
+    v = dot(swap[...], v).astype(BF16)
+    for h in range(2):
+        a[:, ready + 16 * h : ready + 16 * h + 16, :] = v[:, LANES * h : LANES * (h + 1)].reshape(16, 16, LANES)
+    a[:, :ready, :] = a_tail[...]
+    copies = []
+    for g in range(SLOTS // group):
+        at = nt_dot(part_last(), a[group * g : group * (g + 1)].reshape(group * tail, LANES)).astype(BF16)
+        for s in range(group):
+            slot = group * g + s
+            total = acc[slot] + dot(at[:, tail * s : tail * (s + 1)], lp_tail[slot])
+            out[:, slot] = total.astype(BF16).reshape(KEEP, 2, DEG)
+        part = pl.ds(group * g, group)
+        copies.append(pltpu.make_async_copy(out.at[:, part], out_hbm.at[:, part], sems.at[g]))
+        copies[-1].start()
+    for copy in copies:
+        copy.wait()
 
 
 def on_device(grid, legendre, lengths, lat_order, wave_order):
     any_spec = pl.BlockSpec(memory_space=pl.ANY)
-    smem = pl.BlockSpec(memory_space=pltpu.SMEM)
     vmem = pl.BlockSpec(memory_space=pltpu.VMEM)
     n = len(CHUNKS)
     dma = pltpu.SemaphoreType.DMA
-    group = 4
     parts = pl.pallas_call(
         kernel,
         out_shape=[
@@ -372,7 +383,7 @@
             pltpu.VMEM((SLOTS, CUT - HEAD, LANES), BF16),
             pltpu.VMEM((NLAT - CUT, SLOTS, LANES), BF16),
         ],
-        in_specs=[any_spec, any_spec, smem, smem, smem, vmem, vmem],
+        in_specs=[any_spec] * 7,
         out_specs=[vmem] * 4,
         scratch_shapes=[
             pltpu.VMEM((512, ROWS, LANES), BF16),
@@ -389,7 +400,12 @@
             pltpu.VMEM((NLAT, NLAT), BF16),
             pltpu.VMEM((256, 256), BF16),
             pltpu.VMEM((NWAVE, LANES), F32),
-            dma((LEVS,)), dma, dma((n,)), dma((n,)), dma((n,)), dma((n,)),
+            pltpu.SMEM((NLAT,), jnp.int32),
+            pltpu.SMEM((NLAT,), jnp.int32),
+            pltpu.SMEM((NWAVE,), jnp.int32),
+            pltpu.VMEM((4, 128), jnp.int32),
+            pltpu.VMEM((4, 128), jnp.int32),
+            dma((LEVS,)), dma, dma((5,)), dma((n,)), dma((n,)), dma((n,)), dma((n,)),
         ],
         compiler_params=pltpu.CompilerParams(
             collective_id=0, has_side_effects=True, vmem_limit_bytes=51 << 20
@@ -398,11 +414,10 @@
     )(grid, legendre, lengths, lat_order, wave_order, lat_order.reshape(4, 128), wave_order.reshape(4, 128))
     return pl.pallas_call(
         finish,
-        grid=(SLOTS // group,),
         out_shape=jax.ShapeDtypeStruct((KEEP, SLOTS, 2, DEG), BF16),
         in_specs=[vmem] * 4,
-        out_specs=pl.BlockSpec((KEEP, group, 2, DEG), lambda i: (0, i, 0, 0)),
-        scratch_shapes=[pltpu.VMEM((SLOTS, NLAT - HEAD, LANES), BF16), pltpu.VMEM((256, 256), BF16)],
+        out_specs=any_spec,
+        scratch_shapes=[pltpu.VMEM((KEEP, SLOTS, 2, DEG), BF16), pltpu.VMEM((SLOTS, NLAT - HEAD, LANES), BF16), pltpu.VMEM((256, 256), BF16), dma((4,))],
         compiler_params=pltpu.CompilerParams(vmem_limit_bytes=32 << 20),
     )(*parts)
 

time: 68.6 us -> 67.1 us (0.978)
  Pallas kernels: 68.5 us -> 67 us
    pallas_call x1, Pallas kernels: 3.16 us -> 2.36 us  [on_device(): pl.pallas_call(finish, out_shape=jax.ShapeDtypeStruct((KEEP, SLOTS, 2, DE...]
    pallas_call x1, Pallas kernels: 65.4 us -> 64.6 us  [on_device(): pl.pallas_call(kernel, out_shape=[pltpu.VMEM((SLOTS, 2 * KEEP, DEG), F32)...]
where the time goes in v4:
time: 67.1 us; the launch traced here: 67 us
  Pallas kernels  67 us (100%)
    pallas_call x1, Pallas kernels, on_device(): pl.pallas_call(kernel, out_shape=[pltpu.VMEM((SLOTS, 2 * KEEP, DEG), F32)...  64.6 us
    pallas_call x1, Pallas kernels, on_device(): pl.pallas_call(finish, out_shape=jax.ShapeDtypeStruct((KEEP, SLOTS, 2, DE...  2.36 us

profile of v4, /device:TPU:1, one launch (start us, length us, event | category | flops | bytes accessed | tf_op | source)
XLA Modules:
  0.0 67.0 jit_solution(1920992722936257068)
XLA Ops:
  0.0 64.6 %shard_map.55 = (f32[16,128,512]{2,1,0:T(8,128)S(1)}, bf16[16,256,512]{2,1,0:T(8,128)(2,1)S(1)}, bf16[16,224,128]{2,1,0:T(8,128)(2,1)S(1)}, bf16[32,16,128]{2,1,0:T(8,128)(2,1)S(1)}) custom-call(bf16[512,16,128]{2,1,0:T(8,128)(2,1)} %grid_hbm.1, bf16[16,512,512]{2,1,0:T(8,128)(2,1)} %leg_hbm.1, s32[512]{0:T(512)} %len_hbm.1, s32[512]{0:T(512)} %lat_hbm.1, ...), custom_call_target="tpu_custom_call" | custom-call | flops 14000000000 | bytes 14680064 | tf_op jit(solution)/shard_map/pallas_call | solution.py:378
  64.6 2.4 %shard_map.56 = bf16[64,16,2,512]{3,2,1,0:T(2,128)(2,1)} custom-call(f32[16,128,512]{2,1,0:T(8,128)S(1)} %get-tuple-element.9.acc, bf16[16,256,512]{2,1,0:T(8,128)(2,1)S(1)} %get-tuple-element.10.lp_tail, bf16[16,224,128]{2,1,0:T(8,128)(2,1)S(1)} %get-tuple-element.11.a_tail, bf16[32,16,128]{2,1,0:T(8,128)(2,1)S(1)} %get-tuple-element.12.fr), custom_call_target="tpu_custom_call" | custom-call | tf_op jit(solution)/shard_map/pallas_call | solution.py:415

commit v5 on v4

--- a/solution.py
+++ b/solution.py
@@ -19,7 +19,7 @@
 NWAVE = 512
 LANES = 128
 
-CHUNKS = (4, 4, 4, 2, 1, 1)
+CHUNKS = (4, 4, 2, 2, 2, 1, 1)
 STARTS = tuple(sum(CHUNKS[:i]) for i in range(len(CHUNKS)))
 LAST = len(CHUNKS) - 1
 CUT = WAVES * STARTS[LAST]
@@ -324,6 +324,7 @@
     make_table(STARTS[3], ROWS - STARTS[3])
     collect(0)
     arrive(2)
+    arrive(3)
     collect(1)
 
     order = part_last()
@@ -335,7 +336,7 @@
 
     lax.fori_loop(0, SLOTS, sum_first, 0, unroll=4)
 
-    for c in range(3, LAST + 1):
+    for c in range(4, LAST + 1):
         arrive(c)
     for c in range(2, LAST):
         collect(c)

time: 67.1 us -> 66.9 us (level)
  no operation moved by 1% of the time
where the time goes in v5:
time: 66.9 us; the launch traced here: 66.8 us
  Pallas kernels  66.8 us (100%)
    pallas_call x1, Pallas kernels, on_device(): pl.pallas_call(kernel, out_shape=[pltpu.VMEM((SLOTS, 2 * KEEP, DEG), F32)...  64.4 us
    pallas_call x1, Pallas kernels, on_device(): pl.pallas_call(finish, out_shape=jax.ShapeDtypeStruct((KEEP, SLOTS, 2, DE...  2.36 us

profile of v5, /device:TPU:1, one launch (start us, length us, event | category | flops | bytes accessed | tf_op | source)
XLA Modules:
  0.0 66.8 jit_solution(18399528281984293665)
XLA Ops:
  0.0 64.4 %shard_map.55 = (f32[16,128,512]{2,1,0:T(8,128)S(1)}, bf16[16,256,512]{2,1,0:T(8,128)(2,1)S(1)}, bf16[16,224,128]{2,1,0:T(8,128)(2,1)S(1)}, bf16[32,16,128]{2,1,0:T(8,128)(2,1)S(1)}) custom-call(bf16[512,16,128]{2,1,0:T(8,128)(2,1)} %grid_hbm.1, bf16[16,512,512]{2,1,0:T(8,128)(2,1)} %leg_hbm.1, s32[512]{0:T(512)} %len_hbm.1, s32[512]{0:T(512)} %lat_hbm.1, ...), custom_call_target="tpu_custom_call" | custom-call | flops 14000000000 | bytes 14680064 | tf_op jit(solution)/shard_map/pallas_call | solution.py:379
  64.4 2.4 %shard_map.56 = bf16[64,16,2,512]{3,2,1,0:T(2,128)(2,1)} custom-call(f32[16,128,512]{2,1,0:T(8,128)S(1)} %get-tuple-element.9.acc, bf16[16,256,512]{2,1,0:T(8,128)(2,1)S(1)} %get-tuple-element.10.lp_tail, bf16[16,224,128]{2,1,0:T(8,128)(2,1)S(1)} %get-tuple-element.11.a_tail, bf16[32,16,128]{2,1,0:T(8,128)(2,1)S(1)} %get-tuple-element.12.fr), custom_call_target="tpu_custom_call" | custom-call | tf_op jit(solution)/shard_map/pallas_call | solution.py:416
